TPU v7x, 32 devices: a whole 2x2x4 slice. The times are simulated.
32 devices in a mesh: member: 2 (over y), band: 4 (over z), face: 2 (over x), rep: 2 (over core).
Axes of the slice: x: 2, y: 2, z: 4, core: 2. Of those that a mesh axis runs over, the one named last changes fastest.
Arguments:
- grid_latent: bfloat16 [32, 192, 512], P(('member', 'band'), ('face', 'rep')), parts along dimension 0, may hold values from -6 to 6
- mesh_latent: bfloat16 [2048, 512], P(('member', 'band', 'face', 'rep')), parts along dimension 0, may hold values from -6 to 6
- w_grid_send: bfloat16 [512, 512], replicated, may hold values from -0.25 to 0.25
- w_mesh_recv: bfloat16 [512, 512], replicated, may hold values from -0.25 to 0.25
- w_g2m_geom: bfloat16 [4, 512], replicated, may hold values from -3 to 3
- w_g2m_out: bfloat16 [512, 512], replicated, may hold values from -0.25 to 0.25
- g2m_gain: float32 [512], replicated, may hold values from 0.5 to 1.5
- w_node_mesh: bfloat16 [512, 512], replicated, may hold values from -0.25 to 0.25
- w_node_agg: bfloat16 [512, 512], replicated, may hold values from -0.25 to 0.25
- w_node_out: bfloat16 [512, 512], replicated, may hold values from -0.25 to 0.25
- node_gain: float32 [512], replicated, may hold values from 0.5 to 1.5
- w_proc_send: bfloat16 [512, 512], replicated, may hold values from -0.25 to 0.25
- w_proc_recv: bfloat16 [512, 512], replicated, may hold values from -0.25 to 0.25
- w_proc_geom: bfloat16 [4, 512], replicated, may hold values from -3 to 3
- w_proc_out: bfloat16 [512, 512], replicated, may hold values from -0.25 to 0.25
- proc_gain: float32 [512], replicated, may hold values from 0.5 to 1.5
- g2m_sender: int32 [32768], P(('band', 'face', 'rep')), may hold values from 0 to 3071, as said below
- g2m_receiver: int32 [32768], P(('band', 'face', 'rep')), may hold values from 0 to 63
- g2m_geom: bfloat16 [4, 32768], P(None, ('band', 'face', 'rep')), may hold values from -6 to 6
- g2m_count: int32 [16], P(('band', 'face', 'rep')), may hold values from 512 to 2048, as said below
- mesh_receiver: int32 [16384], P(('band', 'face', 'rep')), may hold values from 0 to 63
- mesh_slot: int32 [16384], P(('band', 'face', 'rep')), may hold values from 0 to 15
- send_rows: int32 [256], P(('band', 'face', 'rep')), may hold values from 0 to 63, as said below
- mesh_geom: bfloat16 [4, 16384], P(None, ('band', 'face', 'rep')), may hold values from -6 to 6
- mesh_count: int32 [16], P(('band', 'face', 'rep')), may hold values from 256 to 1024, as said below
Outputs:
- mesh_encoded: bfloat16 [2048, 512], P(('member', 'band', 'face', 'rep')), parts along dimension 0
- mesh_messages: bfloat16 [2048, 512], P(('member', 'band', 'face', 'rep')), parts along dimension 0
There are 2 independent parts, one for each index of `member`. A program takes and returns all parts, laid end to end along the dimension named above; an argument that names none is the same for every part. Nothing has to cross between parts.
Inputs may be any that keep to these rules, and one draw needn't show every extreme that they name: `g2m_sender`: the grid node of a slot of device d lies in d's longitude columns and within 2 latitude rows of d's rows (clipped at the poles). `g2m_count`: devices of the first and last band have exactly 2048 live slots. `mesh_count`: devices of the first and last band have exactly 1024 live slots. `send_rows`: the 2 rows that one device lists for one peer are distinct.
All inputs are finite; a program needn't handle non-finite values.
Results may differ from a plain program's by a relative error of at most 0.0085.
Values may be sent and summed in bfloat16 or wider, within the bound.
A program may use at most 64 MiB of HBM per device.

v0:
```python
import functools

import jax
import jax.numpy as jnp
from jax import lax
from jax.experimental import pallas as pl
from jax.experimental.pallas import tpu as pltpu
from jax.sharding import PartitionSpec as P

RIM = 2
EPSILON = 1e-05
LANES = 128
TILE = 1024
SMALL = 14
BF = jnp.bfloat16
F32 = jnp.float32

GRID_SEND, MESH_RECV, G2M_OUT, NODE_MESH, NODE_AGG, NODE_OUT, PROC_SEND, PROC_RECV, PROC_OUT = range(9)


def dot(a, b, contract=((1,), (0,))):
    return lax.dot_general(a, b, (contract, ((), ())), preferred_element_type=F32)


def silu(v):
    half = 0.5 * v
    return half + half * jnp.tanh(half)


def normalized(y, axis):
    scale = 1.0 / y.shape[axis]
    center = y - jnp.sum(y, axis=axis, keepdims=True) * scale
    spread = jnp.sum(center * center, axis=axis, keepdims=True) * scale
    return center * lax.rsqrt(spread + EPSILON)


def hot(index_row, rows):
    edges = index_row.shape[1]
    return jnp.where(lax.broadcasted_iota(jnp.int32, (rows, edges), 0) == index_row, 1.0, 0.0).astype(BF)


def edge_sum(table_t, out_t, hot_ref, receiver_row, nodes, edges):
    total = None
    for start in range(0, edges, TILE):
        cols = pl.ds(start, TILE)
        hidden = silu(dot(table_t[...], hot_ref[:, cols])).astype(BF)
        message = normalized(dot(out_t[...], hidden), 0).astype(BF)
        part = dot(hot_ref[pl.ds(receiver_row, nodes), cols], message, ((1,), (1,)))
        total = part if total is None else total + part
    return total


def kernel(
    dims,
    grid_hbm, mesh_hbm, w0, w1, w2, w3, w4, w5, w6, w7, w8,
    *rest,
):
    small_hbm, outs, small_v, scratch = (
        rest[:SMALL], rest[SMALL:SMALL + 2], rest[SMALL + 2:2 * SMALL + 2], rest[2 * SMALL + 2:]
    )
    enc_out, msg_out = outs
    (
        wgg, wpg, g2m_gain, node_gain, proc_gain,
        g2m_sender, g2m_receiver, g2m_geom, mesh_receiver, mesh_slot, send_rows, mesh_geom,
        g2m_count, mesh_count,
    ) = small_v
    (
        grid_v, mesh_v, w_v, table, table_t, out_t, hot_g, hot_m, table_m, table_mt, out_mt, send_buf, recv_buf,
        load_sem, small_sem, halo_send, halo_recv, row_send, row_recv,
    ) = scratch
    bands, faces, reps, lat_rows, lon_cols, full_lon = dims
    own, width = grid_v.shape
    nodes = mesh_v.shape[0]
    rim = RIM * lon_cols
    g_edges, m_edges = hot_g.shape[1], hot_m.shape[1]
    listed = send_rows.shape[1]
    peers = bands * faces
    slot_rows = send_buf.shape[0] // peers
    chunks = width // LANES
    band, face, rep = lax.axis_index("band"), lax.axis_index("face"), lax.axis_index("rep")
    me = band * faces + face

    sources = (w0, w1, w2, w3, w4, w5, w6, w7, w8)
    loads = [pltpu.make_async_copy(source, w_v.at[i], load_sem.at[i]) for i, source in enumerate(sources)]
    grid_load = pltpu.make_async_copy(grid_hbm, grid_v, load_sem.at[9])
    mesh_load = pltpu.make_async_copy(mesh_hbm, mesh_v, load_sem.at[10])
    small_loads = [
        pltpu.make_async_copy(source, target, small_sem.at[i])
        for i, (source, target) in enumerate(zip(small_hbm, small_v))
    ]
    grid_load.start()
    loads[0].start()
    for load in small_loads:
        load.start()
    mesh_load.start()
    for load in loads[1:]:
        load.start()

    def peer_id(step):
        other = lax.rem(me + step, peers)
        return {"band": other // faces, "face": other % faces}

    def each_peer(body):
        if peers <= 16:
            for step in range(1, peers):
                body(step)
        else:
            pl.loop(1, peers)(body)

    barrier = pltpu.get_barrier_semaphore()
    each_peer(
        lambda step: pl.semaphore_signal(
            barrier, inc=1, device_id=peer_id(step), device_id_type=pl.DeviceIdType.MESH
        )
    )

    mesh_row = own
    low_row = own + nodes
    high_row = low_row + rim
    geom_row = high_row + rim
    end_row = table.shape[0]

    grid_load.wait()
    loads[GRID_SEND].wait()
    table[pl.ds(0, own), :] = dot(grid_v[...], w_v[GRID_SEND]).astype(BF)

    pl.semaphore_wait(barrier, peers - 1)

    def rim_copy(source_row, target_row, target_band, which):
        return pltpu.make_async_remote_copy(
            src_ref=table.at[pl.ds(source_row, rim)],
            dst_ref=table.at[pl.ds(target_row, rim)],
            send_sem=halo_send.at[which],
            recv_sem=halo_recv.at[which],
            device_id={"band": target_band},
            device_id_type=pl.DeviceIdType.MESH,
        )

    up = rim_copy(own - rim, low_row, lax.rem(band + 1, bands), 0)
    down = rim_copy(0, high_row, lax.rem(band + bands - 1, bands), 1)
    has_up, has_down = band < bands - 1, band > 0

    @pl.when(has_up)
    def _():
        up.start()

    @pl.when(has_down)
    def _():
        down.start()

    @pl.when(band == 0)
    def _():
        table[pl.ds(low_row, rim), :] = jnp.zeros((rim, width), BF)

    @pl.when(band == bands - 1)
    def _():
        table[pl.ds(high_row, rim), :] = jnp.zeros((rim, width), BF)

    for load in small_loads:
        load.wait()

    base = (band * lat_rows - RIM) * full_lon + (face * reps + rep) * lon_cols
    sender = g2m_sender[...] - base
    for lat in range(lat_rows + 2 * RIM):
        if lat < RIM:
            row = low_row + lat * lon_cols
        elif lat < RIM + lat_rows:
            row = (lat - RIM) * lon_cols
        else:
            row = high_row + (lat - RIM - lat_rows) * lon_cols
        hot_g[pl.ds(row, lon_cols), :] = hot(sender - lat * full_lon, lon_cols)
    live = lax.broadcasted_iota(jnp.int32, (1, g_edges), 1) < g2m_count[...]
    hot_g[pl.ds(mesh_row, nodes), :] = hot(jnp.where(live, g2m_receiver[...], -1), nodes)
    hot_g[pl.ds(geom_row, end_row - geom_row), :] = jnp.zeros((end_row - geom_row, g_edges), BF)
    hot_g[pl.ds(geom_row, 4), :] = g2m_geom[...]
    table[pl.ds(geom_row, end_row - geom_row), :] = jnp.zeros((end_row - geom_row, width), BF)
    table[pl.ds(geom_row, 4), :] = wgg[...]

    mesh_load.wait()
    loads[MESH_RECV].wait()
    table[pl.ds(mesh_row, nodes), :] = dot(mesh_v[...], w_v[MESH_RECV]).astype(BF)
    table_t[:, pl.ds(0, low_row)] = table[pl.ds(0, low_row), :].T
    loads[G2M_OUT].wait()
    out_t[...] = w_v[G2M_OUT].T
    loads[NODE_MESH].wait()
    node_input = dot(mesh_v[...], w_v[NODE_MESH])

    @pl.when(has_up)
    def _():
        up.wait_send()
        down.wait_recv()

    @pl.when(has_down)
    def _():
        down.wait_send()
        up.wait_recv()

    table_t[:, pl.ds(low_row, end_row - low_row)] = table[pl.ds(low_row, end_row - low_row), :].T

    g2m_sum = edge_sum(table_t, out_t, hot_g, mesh_row, nodes, g_edges)
    g2m_sum = (g2m_sum * g2m_gain[...]).astype(BF)

    loads[NODE_AGG].wait()
    node_hidden = silu(node_input + dot(g2m_sum, w_v[NODE_AGG])).astype(BF)
    loads[NODE_OUT].wait()
    update = normalized(dot(node_hidden, w_v[NODE_OUT]), 1) * node_gain[...]
    encoded = (mesh_v[...].astype(F32) + update).astype(BF)
    enc_out[...] = encoded

    chosen = dot(hot(send_rows[...], nodes), encoded, ((0,), (0,))).astype(BF)
    loads[PROC_SEND].wait()
    sent = dot(chosen, w_v[PROC_SEND]).astype(BF).astype(F32)
    for chunk in range(chunks):
        send_buf[pl.ds(chunk, listed, stride=chunks), :] = sent[:, chunk * LANES:(chunk + 1) * LANES]

    def row_copy(step):
        other = lax.rem(me + step, peers)
        return pltpu.make_async_remote_copy(
            src_ref=send_buf.at[pl.ds(pl.multiple_of(other * slot_rows, 8), slot_rows)],
            dst_ref=recv_buf.at[pl.ds(pl.multiple_of(me * slot_rows, 8), slot_rows)],
            send_sem=row_send.at[step],
            recv_sem=row_recv.at[step],
            device_id=peer_id(step),
            device_id_type=pl.DeviceIdType.MESH,
        )

    each_peer(lambda step: row_copy(step).start())
    mine = pl.ds(pl.multiple_of(me * slot_rows, 8), slot_rows)
    recv_buf[mine, :] = send_buf[mine, :]

    geom_m = listed + nodes
    end_m = table_m.shape[0]
    hot_m[pl.ds(0, listed), :] = hot(mesh_slot[...], listed)
    live = lax.broadcasted_iota(jnp.int32, (1, m_edges), 1) < mesh_count[...]
    hot_m[pl.ds(listed, nodes), :] = hot(jnp.where(live, mesh_receiver[...], -1), nodes)
    hot_m[pl.ds(geom_m, end_m - geom_m), :] = jnp.zeros((end_m - geom_m, m_edges), BF)
    hot_m[pl.ds(geom_m, 4), :] = mesh_geom[...]
    table_m[pl.ds(geom_m, end_m - geom_m), :] = jnp.zeros((end_m - geom_m, width), BF)
    table_m[pl.ds(geom_m, 4), :] = wpg[...]
    loads[PROC_RECV].wait()
    table_m[pl.ds(listed, nodes), :] = dot(encoded, w_v[PROC_RECV]).astype(BF)
    loads[PROC_OUT].wait()
    out_mt[...] = w_v[PROC_OUT].T

    each_peer(lambda step: row_copy(step).wait())
    for chunk in range(chunks):
        table_m[pl.ds(0, listed), pl.ds(chunk * LANES, LANES)] = recv_buf[
            pl.ds(chunk, listed, stride=chunks), :
        ].astype(BF)
    table_mt[...] = table_m[...].T
    messages = edge_sum(table_mt, out_mt, hot_m, listed, nodes, m_edges)
    msg_out[...] = (messages * proc_gain[...]).astype(BF)


def hand_over(enc_in, msg_in, enc_out, msg_out, sems):
    copies = [
        pltpu.make_async_copy(source, target, sems.at[i])
        for i, (source, target) in enumerate(((enc_in, enc_out), (msg_in, msg_out)))
    ]
    for copy in copies:
        copy.start()
    for copy in copies:
        copy.wait()


def round_up(value, step):
    return (value + step - 1) // step * step


def on_device(
    bands,
    faces,
    reps,
    grid_latent,
    mesh_latent,
    w_grid_send,
    w_mesh_recv,
    w_g2m_geom,
    w_g2m_out,
    g2m_gain,
    w_node_mesh,
    w_node_agg,
    w_node_out,
    node_gain,
    w_proc_send,
    w_proc_recv,
    w_proc_geom,
    w_proc_out,
    proc_gain,
    g2m_sender,
    g2m_receiver,
    g2m_geom,
    g2m_count,
    mesh_receiver,
    mesh_slot,
    send_rows,
    mesh_geom,
    mesh_count,
):
    lat_rows, lon_cols, width = grid_latent.shape
    nodes = mesh_latent.shape[0]
    own = lat_rows * lon_cols
    g_edges, m_edges = g2m_sender.shape[0], mesh_slot.shape[0]
    peers = bands * faces
    listed = send_rows.shape[0]
    full_lon = lon_cols * faces * reps
    g_rows = round_up(own + nodes + 2 * RIM * lon_cols + 4, LANES)
    m_rows = round_up(listed + nodes + 4, LANES)
    row = lambda array: array.reshape(1, array.shape[0])
    hbm, vmem = (pl.BlockSpec(memory_space=space) for space in (pltpu.HBM, pltpu.VMEM))
    small = (
        w_g2m_geom, w_proc_geom, row(g2m_gain), row(node_gain), row(proc_gain),
        row(g2m_sender), row(g2m_receiver), g2m_geom, row(mesh_receiver), row(mesh_slot), row(send_rows), mesh_geom,
        row(g2m_count), row(mesh_count),
    )
    rows_out = jax.ShapeDtypeStruct((nodes, width), BF)
    row_tiles = listed * width // LANES
    held = pl.pallas_call(
        functools.partial(kernel, (bands, faces, reps, lat_rows, lon_cols, full_lon)),
        out_shape=(rows_out, rows_out),
        in_specs=[hbm] * (11 + SMALL),
        out_specs=(vmem, vmem),
        scratch_shapes=[
            *(pltpu.VMEM(array.shape, array.dtype) for array in small),
            pltpu.VMEM((own, width), BF),
            pltpu.VMEM((nodes, width), BF),
            pltpu.VMEM((9, width, width), BF),
            pltpu.VMEM((g_rows, width), BF),
            pltpu.VMEM((width, g_rows), BF),
            pltpu.VMEM((width, width), BF),
            pltpu.VMEM((g_rows, g_edges), BF),
            pltpu.VMEM((m_rows, m_edges), BF),
            pltpu.VMEM((m_rows, width), BF),
            pltpu.VMEM((width, m_rows), BF),
            pltpu.VMEM((width, width), BF),
            pltpu.VMEM((row_tiles, LANES), F32),
            pltpu.VMEM((row_tiles, LANES), F32),
            pltpu.SemaphoreType.DMA((11,)),
            pltpu.SemaphoreType.DMA((SMALL,)),
            pltpu.SemaphoreType.DMA((2,)),
            pltpu.SemaphoreType.DMA((2,)),
            pltpu.SemaphoreType.DMA((peers,)),
            pltpu.SemaphoreType.DMA((peers,)),
        ],
        compiler_params=pltpu.CompilerParams(
            collective_id=0, has_side_effects=True, vmem_limit_bytes=56 * 1024 * 1024
        ),
        name="encode_and_edges",
    )(
        grid_latent.reshape(own, width), mesh_latent,
        w_grid_send, w_mesh_recv, w_g2m_out, w_node_mesh, w_node_agg, w_node_out, w_proc_send, w_proc_recv, w_proc_out,
        *small,
    )
    return pl.pallas_call(
        hand_over,
        out_shape=(rows_out, rows_out),
        in_specs=[vmem, vmem],
        out_specs=(hbm, hbm),
        scratch_shapes=[pltpu.SemaphoreType.DMA((2,))],
        name="hand_over",
    )(*held)


def solution(mesh):
    blocks = P(("member", "band", "face", "rep"), None)
    edges = P(("band", "face", "rep"))
    placed = (
        (P(("member", "band"), ("face", "rep"), None), blocks)
        + (P(),) * 14
        + (edges, edges, P(None, ("band", "face", "rep")), edges, edges, edges, edges)
        + (P(None, ("band", "face", "rep")), edges)
    )
    return jax.shard_map(
        functools.partial(on_device, mesh.shape["band"], mesh.shape["face"], mesh.shape["rep"]),
        mesh=mesh,
        in_specs=placed,
        out_specs=(blocks, blocks),
        check_vma=False,
    )
```

profile of v0, /device:TPU:0, one launch (start us, length us, event | category | flops | bytes accessed | tf_op | source)
XLA Modules:
  0.0 23.4 jit_solution(6212400439805760419)
XLA Ops:
  1.9 19.9 %encode_and_edges.1 = (bf16[64,512]{1,0:T(8,128)(2,1)}, bf16[64,512]{1,0:T(8,128)(2,1)}) custom-call(bf16[192,512]{1,0:T(8,128)(2,1)} %bitcast.13, bf16[64,512]{1,0:T(8,128)(2,1)} %mesh_hbm.1, bf16[512,512]{1,0:T(8,128)(2,1)} %w0.1, bf16[512,512]{1,0:T(8,128)(2,1)} %w1.1, bf16[512,512]{1,0:T(8,128)(2,1)} %w2.1, bf16[512,512]{1,0:T(8,128)(2,1)} %w3.1, ...), custom_call_target="tpu_custom_call" | custom-call | tf_op jit(solution)/shard_map/encode_and_edges/pallas_call | solution.py:318
  21.9 1.5 %hand_over.1 = (bf16[64,512]{1,0:T(8,128)(2,1)}, bf16[64,512]{1,0:T(8,128)(2,1)}) custom-call(bf16[64,512]{1,0:T(8,128)(2,1)} %get-tuple-element.4.enc_in, bf16[64,512]{1,0:T(8,128)(2,1)} %get-tuple-element.5.msg_in), custom_call_target="tpu_custom_call" | custom-call | tf_op jit(solution)/shard_map/hand_over/pallas_call | solution.py:354
where the time goes:
time: 23.6 us; the launch traced here: 23.4 us
  Pallas kernels  21.5 us (91%)
  between operations  1.94 us (8%)
    pallas_call x1, Pallas kernels, on_device(): pl.pallas_call(functools.partial(kernel, (bands, faces, reps, lat_rows, l...  19.9 us
    pallas_call x1, Pallas kernels, on_device(): pl.pallas_call(hand_over, out_shape=(rows_out, rows_out), in_specs=[vmem,...  1.54 us

commit v1 on v0

--- a/solution.py
+++ b/solution.py
@@ -39,11 +39,13 @@
     return jnp.where(lax.broadcasted_iota(jnp.int32, (rows, edges), 0) == index_row, 1.0, 0.0).astype(BF)
 
 
-def edge_sum(table_t, out_t, hot_ref, receiver_row, nodes, edges):
+def edge_sum(table_t, out_t, hot_ref, receiver_row, nodes, edges, early=None, first=0):
     total = None
     for start in range(0, edges, TILE):
         cols = pl.ds(start, TILE)
-        hidden = silu(dot(table_t[...], hot_ref[:, cols])).astype(BF)
+        rest = pl.ds(first, hot_ref.shape[0] - first)
+        mixed = dot(table_t[:, rest], hot_ref[rest, cols])
+        hidden = silu(mixed if early is None else mixed + early[:, cols]).astype(BF)
         message = normalized(dot(out_t[...], hidden), 0).astype(BF)
         part = dot(hot_ref[pl.ds(receiver_row, nodes), cols], message, ((1,), (1,)))
         total = part if total is None else total + part
@@ -65,7 +67,7 @@
         g2m_count, mesh_count,
     ) = small_v
     (
-        grid_v, mesh_v, w_v, table, table_t, out_t, hot_g, hot_m, table_m, table_mt, out_mt, send_buf, recv_buf,
+        grid_v, early, mesh_v, w_v, table, table_t, out_t, hot_g, hot_m, table_m, table_mt, out_mt, send_buf, recv_buf,
         load_sem, small_sem, halo_send, halo_recv, row_send, row_recv,
     ) = scratch
     bands, faces, reps, lat_rows, lon_cols, full_lon = dims
@@ -184,6 +186,9 @@
     out_t[...] = w_v[G2M_OUT].T
     loads[NODE_MESH].wait()
     node_input = dot(mesh_v[...], w_v[NODE_MESH])
+    for start in range(0, g_edges, TILE):
+        cols = pl.ds(start, TILE)
+        early[:, cols] = dot(table_t[:, pl.ds(0, low_row)], hot_g[pl.ds(0, low_row), cols])
 
     @pl.when(has_up)
     def _():
@@ -197,7 +202,7 @@
 
     table_t[:, pl.ds(low_row, end_row - low_row)] = table[pl.ds(low_row, end_row - low_row), :].T
 
-    g2m_sum = edge_sum(table_t, out_t, hot_g, mesh_row, nodes, g_edges)
+    g2m_sum = edge_sum(table_t, out_t, hot_g, mesh_row, nodes, g_edges, early, low_row)
     g2m_sum = (g2m_sum * g2m_gain[...]).astype(BF)
 
     loads[NODE_AGG].wait()
@@ -323,6 +328,7 @@
         scratch_shapes=[
             *(pltpu.VMEM(array.shape, array.dtype) for array in small),
             pltpu.VMEM((own, width), BF),
+            pltpu.VMEM((width, g_edges), F32),
             pltpu.VMEM((nodes, width), BF),
             pltpu.VMEM((9, width, width), BF),
             pltpu.VMEM((g_rows, width), BF),

time: 23.6 us -> 23.2 us (0.983)
  Pallas kernels: 21.5 us -> 21.1 us
    pallas_call x1, Pallas kernels: 19.9 us -> 19.5 us  [on_device(): pl.pallas_call(functools.partial(kernel, (bands, faces, reps, lat_rows, l...]
where the time goes in v1:
time: 23.2 us; the launch traced here: 23 us
  Pallas kernels  21.1 us (91%)
  between operations  1.94 us (8%)
    pallas_call x1, Pallas kernels, on_device(): pl.pallas_call(functools.partial(kernel, (bands, faces, reps, lat_rows, l...  19.5 us
    pallas_call x1, Pallas kernels, on_device(): pl.pallas_call(hand_over, out_shape=(rows_out, rows_out), in_specs=[vmem,...  1.54 us

profile of v1, /device:TPU:0, one launch (start us, length us, event | category | flops | bytes accessed | tf_op | source)
XLA Modules:
  0.0 23.0 jit_solution(10653315174303051963)
XLA Ops:
  1.9 19.5 %encode_and_edges.1 = (bf16[64,512]{1,0:T(8,128)(2,1)}, bf16[64,512]{1,0:T(8,128)(2,1)}) custom-call(bf16[192,512]{1,0:T(8,128)(2,1)} %bitcast.13, bf16[64,512]{1,0:T(8,128)(2,1)} %mesh_hbm.1, bf16[512,512]{1,0:T(8,128)(2,1)} %w0.1, bf16[512,512]{1,0:T(8,128)(2,1)} %w1.1, bf16[512,512]{1,0:T(8,128)(2,1)} %w2.1, bf16[512,512]{1,0:T(8,128)(2,1)} %w3.1, ...), custom_call_target="tpu_custom_call" | custom-call | tf_op jit(solution)/shard_map/encode_and_edges/pallas_call | solution.py:323
  21.5 1.5 %hand_over.1 = (bf16[64,512]{1,0:T(8,128)(2,1)}, bf16[64,512]{1,0:T(8,128)(2,1)}) custom-call(bf16[64,512]{1,0:T(8,128)(2,1)} %get-tuple-element.4.enc_in, bf16[64,512]{1,0:T(8,128)(2,1)} %get-tuple-element.5.msg_in), custom_call_target="tpu_custom_call" | custom-call | tf_op jit(solution)/shard_map/hand_over/pallas_call | solution.py:360
